TPU v7x, 32 devices: a whole 2x2x4 slice. The times are simulated.
32 devices in a mesh: dp: 2 (over x), expert: 16 (over z, y, core).
Axes of the slice: x: 2, y: 2, z: 4, core: 2. Of those that a mesh axis runs over, the one named last changes fastest.
Arguments:
- tokens: bfloat16 [2, 3072, 2048], P(None, ('dp', 'expert')), may hold values from -6 to 6
- segment: int32 [2, 3072], P(None, 'dp'), may hold values from 0 to 2, as said below
- routes: int32 [2, 3072, 6], P(None, ('dp', 'expert')), may hold values from 0 to 15, all different within a row; in each aligned block of 96 rows (0 to 95, 96 to 191, ..., all dimensions but the last counted through in order) at most 96 rows name the same one
- drop_order: int32 [2, 32, 96], P(None, ('dp', 'expert')), may hold values from 0 to 95, each once within a row
- cotangent: bfloat16 [2, 3072, 2048], P(None, ('dp', 'expert')), may hold values from -6 to 6
- attn_gain: bfloat16 [2048], P(('dp', 'expert')), may hold values from 0.5 to 1.5
- query_weight: bfloat16 [2048, 3072], P('dp', 'expert'), may hold values from -0.125 to 0.125
- down_latent: bfloat16 [2048, 576], P(('dp', 'expert')), may hold values from -0.125 to 0.125
- latent_gain: bfloat16 [512], P(('dp', 'expert')), may hold values from 0.5 to 1.5
- up_latent: bfloat16 [512, 4096], P('dp', 'expert'), may hold values from -0.25 to 0.25
- output_weight: bfloat16 [2048, 2048], P('expert', 'dp'), may hold values from -0.5 to 0.5
- ffn_gain: bfloat16 [2048], P(('dp', 'expert')), may hold values from 0.5 to 1.5
- router_weight: bfloat16 [2048, 16], P(('dp', 'expert')), may hold values from -0.0625 to 0.0625
- shared_gate: bfloat16 [2048, 2816], P('dp', 'expert'), may hold values from -0.125 to 0.125
- shared_up: bfloat16 [2048, 2816], P('dp', 'expert'), may hold values from -0.125 to 0.125
- shared_down: bfloat16 [2816, 2048], P('expert', 'dp'), may hold values from -0.109375 to 0.109375
- expert_gate: bfloat16 [16, 2048, 1408], P('expert', 'dp'), may hold values from -0.125 to 0.125
- expert_up: bfloat16 [16, 2048, 1408], P('expert', 'dp'), may hold values from -0.125 to 0.125
- expert_down: bfloat16 [16, 1408, 2048], P('expert', None, 'dp'), may hold values from -0.625 to 0.625
Outputs:
- mixed: float32 [2, 3072, 2048], P(None, ('dp', 'expert'))
- tokens_grad: float32 [2, 3072, 2048], P(None, ('dp', 'expert'))
- attn_gain_grad: float32 [2048], P(('dp', 'expert'))
- query_weight_grad: float32 [2048, 3072], P('dp', 'expert')
- down_latent_grad: float32 [2048, 576], P(('dp', 'expert'))
- latent_gain_grad: float32 [512], P(('dp', 'expert'))
- up_latent_grad: float32 [512, 4096], P('dp', 'expert')
- output_weight_grad: float32 [2048, 2048], P('expert', 'dp')
- ffn_gain_grad: float32 [2048], P(('dp', 'expert'))
- router_weight_grad: float32 [2048, 16], P(('dp', 'expert'))
- shared_gate_grad: float32 [2048, 2816], P('dp', 'expert')
- shared_up_grad: float32 [2048, 2816], P('dp', 'expert')
- shared_down_grad: float32 [2816, 2048], P('expert', 'dp')
- expert_gate_grad: float32 [16, 2048, 1408], P('expert', 'dp')
- expert_up_grad: float32 [16, 2048, 1408], P('expert', 'dp')
- expert_down_grad: float32 [16, 1408, 2048], P('expert', None, 'dp')
Inputs may be any that keep to these rules, and one draw needn't show every extreme that they name: `segment`: in each group of 96 rows of a micro-batch the numbers never fall: a prompt of at least 32 tokens, then 2 continuations of 16 to 32 tokens, the first of exactly 32. `routes`: each row names 6 different experts; within one group of a micro-batch some expert may be named by every row. `drop_order`: each group's entries are a permutation of its 96 rows.
All inputs are finite; a program needn't handle non-finite values.
Results may differ from a plain program's by a relative error of at most 0.02.
Values may be sent and summed in bfloat16 or wider, within the bound.
A program may use at most 384 MiB of HBM per device.

v0:
```python
import math

import jax
import jax.numpy as jnp
from jax import lax
from jax.experimental import pallas as pl
from jax.experimental.pallas import tpu as pltpu
from jax.sharding import PartitionSpec as P

DN = 128
DR = 64
DV = 128
EPS = 1e-06
HIGH = lax.Precision.HIGHEST
F32 = jnp.float32
BF = jnp.bfloat16


def dot(former, latter):
    return jnp.dot(former, latter, preferred_element_type=F32)


def dot_left(former, latter):
    return lax.dot_general(former, latter, (((0,), (0,)), ((), ())), preferred_element_type=F32)


def dot_right(former, latter):
    return lax.dot_general(former, latter, (((1,), (1,)), ((), ())), preferred_element_type=F32)


def rms_scale(values):
    return lax.rsqrt(jnp.mean(values * values, axis=-1, keepdims=True) + EPS)


def norm_back(values, scale_rows, gain, out_grad):
    scaled = out_grad * gain
    inner = jnp.mean(scaled * values, axis=-1, keepdims=True)
    value_grad = scale_rows * scaled - values * scale_rows * scale_rows * scale_rows * inner
    return (value_grad, jnp.sum(out_grad * values * scale_rows, axis=0))


def positions(segment):
    places = jnp.arange(segment.shape[1], dtype=jnp.int32)
    prompt_len = jnp.sum((segment == 0).astype(jnp.int32), axis=1, keepdims=True)
    former = (segment[:, None, :] < segment[:, :, None]).astype(jnp.int32)
    seg_start = jnp.sum(former, axis=2)
    return jnp.where(segment == 0, places[None], prompt_len + places[None] - seg_start)


def angles(position, row_count):
    freq_index = jnp.arange(DR // 2, dtype=F32)
    frequency = jnp.exp(freq_index * (-2.0 * math.log(10000.0) / DR))
    turning = jnp.arange(row_count, dtype=F32)[:, None] * frequency[None, :]
    cosine, sine_part = jnp.cos(turning), jnp.sin(turning)
    table = jnp.concatenate([cosine] * 4 + [-sine_part, sine_part] * 2, axis=1)
    picks = (position.reshape(-1)[:, None] == jnp.arange(row_count)[None, :]).astype(F32)
    return jnp.dot(picks, table, precision=HIGH)


LINE = 4
PIECES = 3
MESH = pl.DeviceIdType.MESH
VMEM_LIMIT = 60 * 1024 * 1024


def place_of(me):
    return (me // 4, lax.rem(me // 2, 2), lax.rem(me, 2))


def index_of(line, pair, core):
    return line * 4 + pair * 2 + core


def greet(line, pair, core, others=0):
    barrier = pltpu.get_barrier_semaphore()

    def signal(target):
        pl.semaphore_signal(barrier, inc=1, device_id={"expert": target}, device_id_type=MESH)

    signal(index_of(line, pair, 1 - core))
    signal(index_of(line, 1 - pair, core))

    @pl.when(line > 0)
    def _():
        signal(index_of(line - 1, pair, core))

    @pl.when(line < LINE - 1)
    def _():
        signal(index_of(line + 1, pair, core))

    inner = jnp.where(line > 0, 1, 0) + jnp.where(line < LINE - 1, 1, 0)
    pl.semaphore_wait(barrier, 2 + others + inner)


def greet_dp(others):
    barrier = pltpu.get_barrier_semaphore()
    me_d, n_d = lax.axis_index("dp"), lax.axis_size("dp")
    if others:
        for step in range(1, n_d):
            pl.semaphore_signal(
                barrier,
                inc=1,
                device_id={"dp": lax.rem(me_d + step, n_d)},
                device_id_type=MESH,
            )


def ride(sources, targets, send_sem, recv_sem, start=True):
    me_d, n_d = lax.axis_index("dp"), lax.axis_size("dp")
    copies = []
    for number, (source, target) in enumerate(zip(sources, targets)):
        parts = len(source.shape) == len(target.shape)
        for step in range(1, n_d):
            copy = pltpu.make_async_remote_copy(
                src_ref=source.at[step - 1] if parts else source,
                dst_ref=target.at[step - 1],
                send_sem=send_sem.at[number, step - 1],
                recv_sem=recv_sem.at[number, step - 1],
                device_id={"dp": lax.rem(me_d + step, n_d)},
                device_id_type=MESH,
            )
            if start:
                copy.start()
            copies.append(copy)
    return copies


def landed(rider):
    array, rows = rider
    if rows is None:
        return jax.ShapeDtypeStruct(array.shape, array.dtype)
    shape = (lax.axis_size("dp") - 1, rows[1] - rows[0]) + array.shape[1:]
    return jax.ShapeDtypeStruct(shape, array.dtype)


def cut_rows(ref, rows):
    return ref if rows is None else ref.at[pl.ds(rows[0], rows[1] - rows[0])]


def when(condition, action):
    if condition is None:
        action()
    else:
        pl.when(condition)(action)


def gather_kernel(spans, products, *refs):
    riders = len(spans)
    take = taker(refs)
    (own_ref,), sources = take(1), take(riders)
    products_in = take(5) if products else None
    (out_ref,), targets = take(1), take(riders)
    products_out = take(7) if products else None
    own_sem, send_sem, recv_sem, ride_send, ride_recv = take(5)
    if products:
        products = ExpertGradients(products_in, products_out, take(12))
    sources = [cut_rows(source, rows) for source, rows in zip(sources, spans)]
    me = lax.axis_index("expert")
    line, pair, core = place_of(me)
    rows = own_ref.shape[0]
    sixth = rows // 6
    half = (rows - sixth) // 2
    spans_of = (pl.ds(0, sixth), pl.ds(sixth, half), pl.ds(sixth + half, half))
    others = lax.axis_size("dp") - 1 if riders or products else 0
    greet_dp(others)
    greet(line, pair, core, others)
    local = [pltpu.make_async_copy(own_ref, out_ref.at[me], own_sem)]
    sent = []

    def push(condition, kind, origin, piece, target, source=None):
        block = out_ref.at[origin, spans_of[piece]]
        copy = pltpu.make_async_remote_copy(
            src_ref=block if source is None else source,
            dst_ref=block,
            send_sem=send_sem.at[kind, origin, piece],
            recv_sem=recv_sem.at[origin, piece],
            device_id={"expert": target},
            device_id_type=MESH,
        )
        when(condition, copy.start)
        sent.append((condition, copy))

    def arrive(condition, origin, piece):
        block = out_ref.at[origin, spans_of[piece]]
        copy = pltpu.make_async_remote_copy(
            src_ref=block,
            dst_ref=block,
            send_sem=send_sem.at[0, origin, piece],
            recv_sem=recv_sem.at[origin, piece],
            device_id={"expert": me},
            device_id_type=MESH,
        )
        when(condition, copy.wait_recv)

    left = index_of(line - 1, pair, core)
    right = index_of(line + 1, pair, core)
    across = index_of(line, 1 - pair, core)
    sibling = index_of(line, pair, 1 - core)
    for piece in range(PIECES):
        source = own_ref.at[spans_of[piece]]
        push(line < LINE - 1, 1, me, piece, right, source)
        push(line > 0, 0, me, piece, left, source)
        push(None, 2, me, piece, across, source)
        push(None, 3, me, piece, sibling, source)
    ridden = ride(sources, targets, ride_send, ride_recv)
    for copy in local:
        copy.start()
    if products:
        products.load()

    def work():
        if products:
            products.next()

    def along(hop, piece):
        for side in (-1, 1):
            there = line + side * hop
            held = (there >= 0) & (there < LINE)
            origin = index_of(there, pair, core)
            arrive(held, origin, piece)
            pass_on(held, side, hop, origin, piece)
            if piece:
                push(held, 2, origin, piece, across)
            push(held, 3, origin, piece, sibling)
        work()

    def pass_on(held, side, hop, origin, piece):
        if hop < LINE - 1:
            further = held & ((line < LINE - 1) if side < 0 else (line > 0))
            kind, target = (1, right) if side < 0 else (0, left)
            push(further, kind, origin, piece, target)

    def over(hop, piece):
        for side in (-1, 1) if hop else (1,):
            there = line + side * hop
            held = (there >= 0) & (there < LINE) if hop else None
            origin = index_of(there, 1 - pair, core)
            arrive(held, origin, piece)
            if piece == 0 and hop:
                pass_on(held, side, hop, origin, piece)
            if piece == 0 and not hop:
                push(line < LINE - 1, 1, origin, piece, right)
                push(line > 0, 0, origin, piece, left)
            push(held, 3, origin, piece, sibling)
        work()

    over(0, 0)
    for hop in range(1, LINE):
        for piece in range(PIECES):
            along(hop, piece)
        over(hop, 0)
        for piece in range(1, PIECES):
            over(hop - 1, piece)
    for piece in range(1, PIECES):
        over(LINE - 1, piece)
    for other_line in range(LINE):
        for other_pair in range(2):
            for piece in range(PIECES):
                arrive(None, index_of(other_line, other_pair, 1 - core), piece)
    if products:
        products.finish()
    for copy in ridden:
        copy.wait()
    for condition, copy in sent:
        when(condition, copy.wait_send)
    for copy in local:
        copy.wait()


class ExpertGradients:

    def __init__(self, operands, outs, scratch):
        self.sources = operands
        self.nows, self.landing, self.laters = outs[:3], outs[3:5], outs[5:7]
        self.held = scratch[:5]
        self.lows, self.stage = scratch[5:8], scratch[8]
        self.load_sem, self.out_sem, self.ride_sem = scratch[9:12]
        self.me_d, self.n_d = lax.axis_index("dp"), lax.axis_size("dp")
        self.pending, self.riding, self.count = [None, None], [], 0
        self.kinds = ((2, 1, 1), (0, 3, 0), (0, 4, 0))
        self.steps = self.all_steps()

    def load(self):
        self.loads = [
            pltpu.make_async_copy(source, held, self.load_sem.at[number])
            for number, (source, held) in enumerate(zip(self.sources, self.held))
        ]
        for copy in self.loads:
            copy.start()

    def chunk(self, number, owner, at):
        left, right, axis = self.kinds[number]
        left, right = self.held[left], self.held[right]
        shape = self.nows[number].shape
        count = chunk_rows(number, shape[0])
        if axis == 0:
            first = pl.multiple_of(owner * shape[0] + at * count, 128)
            return dot_left(left[:, pl.ds(first, count)], right[...])
        columns = pl.ds(pl.multiple_of(owner * shape[1], 128), shape[1])
        return dot_left(left[:, at * count : (at + 1) * count], right[:, columns])

    def all_steps(self):
        for copy in self.loads:
            copy.wait()
        for number in range(3):
            shape = self.nows[number].shape
            count = chunk_rows(number, shape[0])
            low = self.lows[number]
            for ahead in range(1, self.n_d):
                owner = lax.rem(self.me_d + ahead, self.n_d)
                for at in range(shape[0] // count):
                    low[ahead - 1, at * count : (at + 1) * count] = self.chunk(
                        number, owner, at
                    ).astype(BF)
                    if number == 1 and (at + 1) * count == shape[0] // 2:
                        self.leave(number, ahead, low.at[ahead - 1, : shape[0] // 2])
                    if at == shape[0] // count - 1:
                        first = shape[0] // 2 if number == 1 else 0
                        self.leave(2 + number // 2 if number else 0, ahead, low.at[ahead - 1, first:])
                    yield
        for number in range(3):
            shape = self.nows[number].shape
            count = chunk_rows(number, shape[0])
            for at in range(shape[0] // count):
                slot = self.count % 2
                if self.pending[slot] is not None:
                    self.pending[slot].wait()
                stage = self.stage.at[slot, :count, : shape[1]]
                stage[...] = self.chunk(number, self.me_d, at)
                copy = pltpu.make_async_copy(
                    stage,
                    self.nows[number].at[pl.ds(at * count, count)],
                    self.out_sem.at[slot],
                )
                copy.start()
                self.pending[slot] = copy
                self.count += 1
                yield

    def leave(self, kind, ahead, source):
        if kind >= 2:
            copy = pltpu.make_async_copy(
                source,
                self.laters[kind - 2].at[ahead - 1],
                self.load_sem.at[3 + 2 * ahead + kind - 2],
            )
        else:
            copy = pltpu.make_async_remote_copy(
                src_ref=source,
                dst_ref=self.landing[kind].at[ahead - 1],
                send_sem=self.ride_sem.at[0, kind, ahead - 1],
                recv_sem=self.ride_sem.at[1, kind, ahead - 1],
                device_id={"dp": lax.rem(self.me_d + ahead, self.n_d)},
                device_id_type=MESH,
            )
        copy.start()
        self.riding.append(copy)

    def next(self):
        next(self.steps, None)

    def finish(self):
        for _ in self.steps:
            pass
        for copy in self.riding + [copy for copy in self.pending if copy is not None]:
            copy.wait()


def chunk_rows(number, rows):
    return rows // 4 if number == 0 else min(256, rows // 2)


def gradient_shapes(products, n_d):
    rows, ups, scaled, gate, up = products
    width, hidden = rows.shape[1], gate.shape[1]
    size = width // n_d
    nows = [(hidden, size), (size, hidden), (size, hidden)]
    shapes = [jax.ShapeDtypeStruct(shape, F32) for shape in nows]
    sent = [nows[0], (size // 2, hidden), (size // 2, hidden), nows[2]]
    shapes += [jax.ShapeDtypeStruct((n_d - 1,) + shape, BF) for shape in sent]
    largest = max(hidden, size)
    scratch = [pltpu.VMEM(product.shape, BF) for product in products]
    scratch += [pltpu.VMEM((n_d - 1,) + shape, BF) for shape in nows]
    scratch += [
        pltpu.VMEM((2, 384, largest), F32),
        pltpu.SemaphoreType.DMA((5 + 2 * n_d,)),
        pltpu.SemaphoreType.DMA((2,)),
        pltpu.SemaphoreType.DMA((2, 3, n_d - 1)),
    ]
    return (shapes, scratch)


def gather_rows(own, collective_id, riders=(), products=()):
    count = lax.axis_size("expert")
    rows, width = own.shape
    shapes = [jax.ShapeDtypeStruct((count, rows, width), own.dtype)]
    shapes += [landed(rider) for rider in riders]
    n_d = lax.axis_size("dp")
    carried, others = max(1, len(riders)), max(1, n_d - 1)
    scratch = []
    if products:
        extra_shapes, scratch = gradient_shapes(products, n_d)
        shapes += extra_shapes
    out = pl.pallas_call(
        lambda *refs: gather_kernel([rider[1] for rider in riders], bool(products), *refs),
        out_shape=shapes,
        in_specs=[pl.BlockSpec(memory_space=pl.ANY)] * (1 + len(riders) + len(products)),
        out_specs=[pl.BlockSpec(memory_space=pl.ANY)] * len(shapes),
        scratch_shapes=[
            pltpu.SemaphoreType.DMA,
            pltpu.SemaphoreType.DMA((4, count, PIECES)),
            pltpu.SemaphoreType.DMA((count, PIECES)),
            pltpu.SemaphoreType.DMA((carried, others)),
            pltpu.SemaphoreType.DMA((carried, others)),
        ]
        + scratch,
        compiler_params=pltpu.CompilerParams(
            collective_id=collective_id, has_side_effects=True, vmem_limit_bytes=VMEM_LIMIT
        ),
        name="gather_rows",
    )(own, *[rider[0] for rider in riders], *products)
    return [out[0].reshape(count * rows, width)] + list(out[1:])


FAR_FIRST = ((3, 3, 0, 0), (2, 0, 3, 1), (1, 2, 1, 2), (0, 1, 2, 3))
COLUMNS = 512
STRIP = 16
EXTRA_ROWS = 48


def pick_by(line, table):
    value = jnp.int32(table[LINE - 1])
    for k in range(LINE - 2, -1, -1):
        value = jnp.where(line == k, jnp.int32(table[k]), value)
    return value


def add_strips(target, first, count, others):
    @pl.loop(0, count // STRIP)
    def _(strip):
        for columns in range(0, target.shape[1], COLUMNS):
            at = pl.ds(pl.multiple_of(first + strip * STRIP, STRIP), STRIP)
            cols = pl.ds(columns, COLUMNS)
            total = None
            for other in others:
                term = other[at, cols].astype(F32)
                total = term if total is None else total + term
            target[at, cols] = total.astype(target.dtype)


def step_scatter(step, buffers, semaphores):
    part, kept, met, paired, passed = buffers
    core_send, core_recv, pair_send, pair_recv, line_send, line_recv = semaphores
    me = lax.axis_index("expert")
    line, pair, core = place_of(me)
    rows = kept.shape[0]
    piece_rows = rows // PIECES
    sibling = index_of(line, pair, 1 - core)
    across = index_of(line, 1 - pair, core)
    steps = 2 * LINE

    def remote(source, dest, send_at, recv_at, target):
        return pltpu.make_async_remote_copy(
            src_ref=source,
            dst_ref=dest,
            send_sem=send_at,
            recv_sem=recv_at,
            device_id={"expert": target},
            device_id_type=MESH,
        )

    def to_sibling(i):
        return remote(part, met.at[i], core_send.at[i], core_recv.at[i], sibling)

    def to_pair(i, piece):
        at = pl.ds(piece * piece_rows, piece_rows)
        return remote(
            met.at[i, at],
            paired.at[i // 2, at],
            pair_send.at[i // 2, piece],
            pair_recv.at[i // 2, piece],
            across,
        )

    def meet(i):
        to_sibling(i).wait_recv()
        add_strips(met.at[i], 0, rows, [met.at[i], kept])

        @pl.when(lax.rem(i, 2) == 0)
        def _():
            for piece in range(PIECES):
                to_pair(i, piece).start()

    dest_line = [pick_by(line, FAR_FIRST[k]) for k in range(LINE)]

    def hop_facts(k):
        there = dest_line[k]
        way = jnp.where(there > line, 1, -1)
        behind = line - way
        held = (behind >= 0) & (behind < LINE)
        slot = jnp.where((there == line + way) & (way < 0), LINE, there)
        return (there, held, slot, index_of(line + way, pair, core))

    def along(k, piece):
        there, held, slot, target = hop_facts(k)
        at = pl.ds(piece * piece_rows, piece_rows)
        return remote(
            paired.at[k, at],
            passed.at[slot, at],
            line_send.at[k, piece],
            line_recv.at[slot, piece],
            target,
        )

    def came_along(slot, piece):
        at = pl.ds(piece * piece_rows, piece_rows)
        block = passed.at[slot, at]
        remote(block, block, line_send.at[0, piece], line_recv.at[slot, piece], me).wait_recv()

    def pair_arrived(k, piece):
        at = pl.ds(piece * piece_rows, piece_rows)
        block = paired.at[k, at]
        remote(block, block, pair_send.at[k, piece], pair_recv.at[k, piece], me).wait_recv()

    def hop(k, with_held):
        there = hop_facts(k)[0]
        for piece in range(PIECES):
            first = piece * piece_rows
            pair_arrived(k, piece)
            terms = [paired.at[k], met.at[2 * k + 1]]
            if with_held:
                came_along(there, piece)
                terms.append(passed.at[there])
            add_strips(paired.at[k], first, piece_rows, terms)
            along(k, piece).start()

    def advance(produce):
        @pl.when(step > 0)
        def _():
            meet(step - 1)

        for k in range(LINE - 1):
            held = hop_facts(k)[1]
            if 2 * k + 3 < steps:

                @pl.when((step == 2 * k + 3) & jnp.logical_not(held))
                def _():
                    hop(k, False)

            if 2 * k + 4 < steps:

                @pl.when((step == 2 * k + 4) & held)
                def _():
                    hop(k, True)

        @pl.when(step > 0)
        def _():
            to_sibling(step - 1).wait_send()

        for which in range(2):

            @pl.when(core == which)
            def _():
                produce((1 - which) * rows, part)

        to_sibling(step).start()
        for which in range(2):

            @pl.when(core == which)
            def _():
                produce(which * rows, kept)

    def finish(sum_ref):
        last_hop()
        last_sum(sum_ref)

    def last_hop():
        meet(steps - 1)
        last = LINE - 2

        @pl.when(hop_facts(last)[1])
        def _():
            hop(last, True)

    def last_sum(sum_ref):
        for piece in range(PIECES):
            first = piece * piece_rows
            pair_arrived(LINE - 1, piece)
            add_strips(
                sum_ref, first, piece_rows, [paired.at[LINE - 1], met.at[2 * LINE - 1]]
            )
            for has, slot in ((line > 0, line), (line < LINE - 1, LINE)):

                @pl.when(has)
                def _():
                    came_along(slot, piece)
                    add_strips(sum_ref, first, piece_rows, [sum_ref, passed.at[slot]])

        to_sibling(steps - 1).wait_send()
        for piece in range(PIECES):
            for k in range(LINE):
                to_pair(2 * k, piece).wait_send()
            for k in range(LINE - 1):
                along(k, piece).wait_send()

    return (advance, finish, last_hop, last_sum)


def step_buffers(block):
    return [
        pltpu.VMEM(block, BF),
        pltpu.VMEM(block, BF),
        pltpu.VMEM((2 * LINE,) + block, BF),
        pltpu.VMEM((LINE,) + block, BF),
        pltpu.VMEM((LINE + 1,) + block, BF),
        pltpu.SemaphoreType.DMA((2 * LINE,)),
        pltpu.SemaphoreType.DMA((2 * LINE,)),
        pltpu.SemaphoreType.DMA((LINE, PIECES)),
        pltpu.SemaphoreType.DMA((LINE, PIECES)),
        pltpu.SemaphoreType.DMA((LINE, PIECES)),
        pltpu.SemaphoreType.DMA((LINE + 1, PIECES)),
    ]


def step_tile(i):
    line, pair, _ = place_of(lax.axis_index("expert"))
    there = pick_by(line, FAR_FIRST[LINE - 1])
    for k in range(LINE - 2, -1, -1):
        there = jnp.where(i // 2 == k, pick_by(line, FAR_FIRST[k]), there)
    return there * 2 + jnp.where(lax.rem(i, 2) == 0, 1 - pair, pair)


def taker(refs):
    refs = list(refs)

    def take(number):
        taken = refs[:number]
        del refs[:number]
        return taken

    return take


def scatter_folded(fold, out_ref, buffers, semaphores):
    part, met, paired, passed = buffers
    core_send, core_recv, pair_send, pair_recv, line_send, line_recv = semaphores
    me = lax.axis_index("expert")
    line, pair, core = place_of(me)
    rows = out_ref.shape[0]
    sibling = index_of(line, pair, 1 - core)
    across = index_of(line, 1 - pair, core)
    sent = []

    def send(source, dest, send_at, recv_at, target):
        copy = pltpu.make_async_remote_copy(
            src_ref=source,
            dst_ref=dest,
            send_sem=send_at,
            recv_sem=recv_at,
            device_id={"expert": target},
            device_id_type=MESH,
        )
        copy.start()
        sent.append(copy)

    def await_block(block, recv_at, send_at):
        pltpu.make_async_remote_copy(
            src_ref=block,
            dst_ref=block,
            send_sem=send_at,
            recv_sem=recv_at,
            device_id={"expert": me},
            device_id_type=MESH,
        ).wait_recv()

    dest_line = [pick_by(line, FAR_FIRST[step]) for step in range(LINE)]

    def chip(i):
        return (dest_line[i // 2], (1 - pair) if i % 2 == 0 else pair)

    for i in range(2 * LINE):
        there, other = chip(i)
        fold(index_of(there, other, 1 - core), part.at[i])
        send(part.at[i], met.at[i], core_send.at[i], core_recv.at[i], sibling)
    for i in range(2 * LINE):
        there, other = chip(i)
        await_block(met.at[i], core_recv.at[i], core_send.at[i])
        fold(index_of(there, other, core), paired.at[LINE])
        add_strips(met.at[i], 0, rows, [met.at[i], paired.at[LINE]])
        if i % 2 == 0:
            send(met.at[i], paired.at[i // 2], pair_send.at[i // 2], pair_recv.at[i // 2], across)
    for step in range(LINE - 1):
        there = dest_line[step]
        way = jnp.where(there > line, 1, -1)
        behind = line - way
        held = (behind >= 0) & (behind < LINE)
        target = index_of(line + way, pair, core)
        slot = jnp.where((there == line + way) & (way < 0), LINE, there)
        await_block(paired.at[step], pair_recv.at[step], pair_send.at[step])
        add_strips(paired.at[step], 0, rows, [paired.at[step], met.at[2 * step + 1]])

        @pl.when(held)
        def _():
            await_block(passed.at[there], line_recv.at[there], line_send.at[step])
            add_strips(paired.at[step], 0, rows, [paired.at[step], passed.at[there]])

        send(paired.at[step], passed.at[slot], line_send.at[step], line_recv.at[slot], target)
    step = LINE - 1
    await_block(paired.at[step], pair_recv.at[step], pair_send.at[step])
    add_strips(out_ref, 0, rows, [paired.at[step], met.at[2 * step + 1]])
    for held, slot in ((line > 0, line), (line < LINE - 1, LINE)):

        @pl.when(held)
        def _():
            await_block(passed.at[slot], line_recv.at[slot], line_send.at[0])
            add_strips(out_ref, 0, rows, [out_ref, passed.at[slot]])

    for copy in sent:
        copy.wait_send()


TILE_GROUPS = 4
SCALE = (DN + DR) ** (-0.5)


def half_turn(values):
    lane = lax.broadcasted_iota(jnp.int32, values.shape, 1)
    lower = (lane // (DR // 2)) % 2 == 0
    return jnp.where(lower, pltpu.roll(values, 128 - DR // 2, 1), pltpu.roll(values, DR // 2, 1))


def group_mask(column_ref, row_ref):
    column, row = column_ref[...], row_ref[0]
    shape = (column.shape[0], row.shape[1])
    earlier = lax.broadcasted_iota(jnp.int32, shape, 1) <= lax.broadcasted_iota(
        jnp.int32, shape, 0
    )
    same = (column == row) | ((row % 4 == 0) & (column // 4 == row // 4))
    return earlier & same


def softmax_scores(query, key, mask):
    scores = jnp.where(mask, dot_right(query, key) * SCALE, -1e30)
    powers = jnp.exp(scores - jnp.max(scores, axis=-1, keepdims=True))
    return powers / jnp.sum(powers, axis=-1, keepdims=True)


def attention_forward_kernel(
    spans, x_ref, gain_ref, first_ref, latent_gain_ref, up_ref, trig_ref, column_ref, row_ref,
    output_ref, *refs,
):
    riders = len(spans)
    take = taker(refs)
    sources = [cut_rows(source, rows) for source, rows in zip(take(riders), spans)]
    normed_ref, query_ref, key_ref, value_ref, unit_ref, low_ref, scale_ref, attended_ref = take(8)
    (sum_ref,), targets = take(1), take(riders)
    buffers, semaphores, ride_sems = take(5), take(6), take(2)
    step = pl.program_id(0)

    @pl.when(step == 0)
    def _():
        others = lax.axis_size("dp") - 1 if riders else 0
        greet_dp(others)
        greet(*place_of(lax.axis_index("expert")), others)
        ride(sources, targets, *ride_sems)

    rank = up_ref.shape[0]
    inputs = x_ref[...].astype(F32)
    scale = lax.rsqrt(jnp.mean(inputs * inputs, axis=1, keepdims=True) + EPS)
    normed_ref[...] = (inputs * scale * gain_ref[...]).astype(BF)
    out = dot(normed_ref[...], first_ref[...])
    latent = out[:, DN : DN + rank]
    latent_scale = lax.rsqrt(jnp.mean(latent * latent, axis=1, keepdims=True) + EPS)
    scale_ref[...] = latent_scale
    unit = latent * latent_scale
    unit_ref[...] = unit.astype(BF)
    low_ref[...] = (unit * latent_gain_ref[...]).astype(BF)
    keys_values = dot(low_ref[...], up_ref[...])
    rope = out[:, DN + rank :]
    turned = rope * trig_ref[:, :128] + half_turn(rope) * trig_ref[:, 128:]
    lane = lax.broadcasted_iota(jnp.int32, turned.shape, 1)
    query_ref[:, :DN] = out[:, :DN].astype(BF)
    query_ref[:, DN:] = jnp.where(lane < DR, pltpu.roll(turned, DR, 1), 0.0).astype(BF)
    key_ref[:, :DN] = keys_values[:, :DN].astype(BF)
    key_ref[:, DN:] = jnp.where(lane < DR, turned, 0.0).astype(BF)
    value_ref[...] = keys_values[:, DN:].astype(BF)
    probs = softmax_scores(query_ref[...], key_ref[...], group_mask(column_ref, row_ref))
    attended_ref[...] = dot(probs.astype(BF), value_ref[...]).astype(BF)
    advance, finish, _, _ = step_scatter(step, buffers, semaphores)

    def produce(first, target):
        rows, width = target.shape

        @pl.loop(0, width // COLUMNS)
        def _(tile):
            columns = pl.ds(pl.multiple_of(tile * COLUMNS, COLUMNS), COLUMNS)
            target[:, columns] = dot(
                attended_ref[pl.ds(first, rows)], output_ref[:, columns]
            ).astype(BF)

    advance(produce)

    @pl.when(step == 2 * LINE - 1)
    def _():
        finish(sum_ref)
        for copy in ride(sources, targets, *ride_sems, start=False):
            copy.wait()


def attention_forward(
    x, gain, first_w, latent_gain, up_w, trig, column, row, output_w, riders, collective_id
):
    width, rank = first_w.shape[0], up_w.shape[0]
    span, rows = column.shape[0], row.shape[2]

    def tile(columns):
        return pl.BlockSpec((rows, columns), lambda i: (step_tile(i), 0))

    def fixed(shape):
        return pl.BlockSpec(shape, lambda i: (0, 0), pipeline_mode=pl.Buffered(1))

    anywhere = pl.BlockSpec(memory_space=pl.ANY)
    block = (rows // 2, width)
    carried, others = max(1, len(riders)), max(1, lax.axis_size("dp") - 1)
    outs = (width, 2 * DN, 2 * DN, DV, rank, rank, 1, DV)
    kinds = (BF, BF, BF, BF, BF, BF, F32, BF)
    return pl.pallas_call(
        lambda *refs: attention_forward_kernel([rider[1] for rider in riders], *refs),
        grid=(span // rows,),
        in_specs=[
            tile(width),
            fixed((1, width)),
            fixed(first_w.shape),
            fixed((1, rank)),
            fixed(up_w.shape),
            tile(trig.shape[1]),
            tile(1),
            pl.BlockSpec((1, 1, rows), lambda i: (step_tile(i), 0, 0)),
            fixed(output_w.shape),
        ]
        + [anywhere] * len(riders),
        out_specs=[tile(columns) for columns in outs]
        + [pl.BlockSpec(block, lambda i: (0, 0))]
        + [anywhere] * len(riders),
        out_shape=[jax.ShapeDtypeStruct((span, c), k) for c, k in zip(outs, kinds)]
        + [jax.ShapeDtypeStruct(block, F32)]
        + [landed(rider) for rider in riders],
        scratch_shapes=step_buffers(block)
        + [pltpu.SemaphoreType.DMA((carried, others)) for _ in range(2)],
        compiler_params=pltpu.CompilerParams(
            collective_id=collective_id, has_side_effects=True, vmem_limit_bytes=VMEM_LIMIT
        ),
        name="attention_forward",
    )(
        x, gain[None], first_w, latent_gain[None], up_w, trig, column, row, output_w,
        *[rider[0] for rider in riders],
    )


def attention_backward_kernel(
    latent_piece, small_rows, spans,
    r_ref, output_ref, attended_ref, query_ref, key_ref, value_ref, column_ref, row_ref, trig_ref,
    unit_ref, low_ref, scale_ref, latent_gain_ref, up_ref, normed_ref, first_ref,
    side_ref, gain_ref, down_now_ref, down_parts_ref, *refs,
):
    riders = len(spans)
    take = taker(refs)
    sources = [cut_rows(source, rows) for source, rows in zip(take(riders), spans)]
    (sum_ref, folded_ref, down_ref), (query_out, up_out, output_out) = take(3), take(3)
    own_targets, targets = take(4), take(riders)
    grad_ref, kv_ref, output_grad_ref, up_grad_ref, first_grad_ref, gain_grad_ref = take(6)
    query_full, query_low, up_low, output_low, small_ref, folded_low = take(6)
    fold_buffers, fold_semaphores = take(4), take(6)
    buffers, semaphores, ride_sems, out_sem, own_sems = take(5), take(6), take(2), take(1)[0], take(2)
    step = pl.program_id(0)
    rank = up_ref.shape[0]
    n_d, me_d = lax.axis_size("dp"), lax.axis_index("dp")
    experts = lax.axis_size("expert")

    @pl.when(step == 0)
    def _():
        greet_dp(n_d - 1)
        greet(*place_of(lax.axis_index("expert")), n_d - 1)
        ride(sources, targets, *ride_sems)
        output_grad_ref[...] = jnp.zeros_like(output_grad_ref)
        up_grad_ref[...] = jnp.zeros_like(up_grad_ref)
        first_grad_ref[...] = jnp.zeros_like(first_grad_ref)
        gain_grad_ref[...] = jnp.zeros_like(gain_grad_ref)

    down_total = down_now_ref[...]
    for ahead in range(1, n_d):
        down_total = down_total + down_parts_ref[ahead - 1].astype(F32)
    down_ref[...] = down_total
    attended_grad = dot_right(r_ref[...], output_ref[...]).astype(BF)
    output_grad_ref[...] += dot_left(attended_ref[...], r_ref[...])
    probs = softmax_scores(query_ref[...], key_ref[...], group_mask(column_ref, row_ref))
    kv_ref[:, DN:] = dot_left(probs.astype(BF), attended_grad).astype(BF)
    probs_grad = dot_right(attended_grad, value_ref[...])
    inner = jnp.sum(probs * probs_grad, axis=1, keepdims=True)
    score_grad = (probs * (probs_grad - inner)).astype(BF)
    query_grad = dot(score_grad, key_ref[...]) * SCALE
    key_grad = dot_left(score_grad, query_ref[...]) * SCALE
    kv_ref[:, :DN] = key_grad[:, :DN].astype(BF)
    grad_ref[:, :DN] = query_grad[:, :DN].astype(BF)
    rope = key_grad[:, DN:] + pltpu.roll(query_grad[:, DN:], DR, 1)
    rope = rope * trig_ref[:, :128] + half_turn(rope * trig_ref[:, 128:])
    grad_ref[:, DN + rank :] = rope.astype(BF)
    out_grad = dot_right(kv_ref[...], up_ref[...])
    unit = unit_ref[...].astype(F32)
    gain_grad_ref[...] += jnp.sum(out_grad * unit, axis=0, keepdims=True)
    scaled = out_grad * latent_gain_ref[...]
    inner = jnp.mean(scaled * unit, axis=1, keepdims=True)
    grad_ref[:, DN : DN + rank] = (scale_ref[...] * (scaled - unit * inner)).astype(BF)
    up_grad_ref[...] += dot_left(low_ref[...], kv_ref[...])
    first_grad_ref[...] += dot_left(normed_ref[...], grad_ref[...])
    advance, _, last_hop, last_sum = step_scatter(step, buffers, semaphores)

    def produce(first, target):
        rows, width = target.shape

        @pl.loop(0, width // COLUMNS)
        def _(tile):
            columns = pl.ds(pl.multiple_of(tile * COLUMNS, COLUMNS), COLUMNS)
            target[:, columns] = dot_right(
                grad_ref[pl.ds(first, rows)], first_ref[columns, :]
            ).astype(BF)

    advance(produce)

    def part(array, number, owner):
        size = array.shape[1 if number == 2 else 0] // n_d
        at = pl.ds(pl.multiple_of(owner * size, size), size)
        return array.at[:, at] if number == 2 else array.at[at]

    def own_copies():
        copies = []
        for number, low in enumerate((query_low, up_low, output_low)):
            for ahead in range(1, n_d):
                owner = lax.rem(me_d + ahead, n_d)
                copies.append((part(low, number, owner), number, ahead))
        for ahead in range(1, n_d):
            copies.append((folded_low, 3, ahead))
        return [
            pltpu.make_async_remote_copy(
                src_ref=source,
                dst_ref=own_targets[number].at[ahead - 1],
                send_sem=own_sems[0].at[number, ahead - 1],
                recv_sem=own_sems[1].at[number, ahead - 1],
                device_id={"dp": lax.rem(me_d + ahead, n_d)},
                device_id_type=MESH,
            )
            for source, number, ahead in copies
        ]

    @pl.when(step == 2 * LINE - 1)
    def _():
        last = DN + rank
        strip = 256

        @pl.loop(0, first_grad_ref.shape[0] // strip)
        def _(tile):
            first = pl.multiple_of(tile * strip, strip)
            at = pl.ds(first, strip)
            sums = first_grad_ref[at]
            rope = sums[:, last:]
            query_full[at, :DN] = sums[:, :DN]
            query_full[at, DN:] = pltpu.roll(rope, DR, 1)
            query_low[at, :DN] = sums[:, :DN].astype(BF)
            query_low[at, DN:] = pltpu.roll(rope, DR, 1).astype(BF)
            small_ref[at, :rank] = sums[:, DN:last].astype(BF)
            gain_sum = jnp.sum(sums * first_ref[at].astype(F32), axis=1, keepdims=True)
            gain_sum = gain_sum / gain_ref[at]
            row = lax.broadcasted_iota(jnp.int32, (strip, rank), 0) + first
            index = lax.broadcasted_iota(jnp.int32, (strip, rank), 1)
            place = (index // latent_piece) * small_rows + index % latent_piece
            latent_sum = jnp.sum(
                jnp.where(row == place, gain_grad_ref[...], 0.0), axis=1, keepdims=True
            )
            lane = lax.broadcasted_iota(jnp.int32, rope.shape, 1)
            mixed = jnp.where(lane < DR, rope, side_ref[at].astype(F32))
            mixed = jnp.where(lane == DR + experts + 1, gain_sum, mixed)
            mixed = jnp.where(lane == DR + experts + 2, latent_sum, mixed)
            small_ref[at, rank:] = mixed.astype(BF)

        up_low[...] = up_grad_ref[...].astype(BF)
        output_low[...] = output_grad_ref[...].astype(BF)
        outs = [
            pltpu.make_async_copy(query_full, query_out, out_sem.at[0]),
            pltpu.make_async_copy(up_grad_ref, up_out, out_sem.at[1]),
            pltpu.make_async_copy(output_grad_ref, output_out, out_sem.at[2]),
        ]
        for copy in outs:
            copy.start()
        moves = own_copies()
        for copy in moves[: 3 * (n_d - 1)]:
            copy.start()

        def fold(dest, target):
            wide = small_ref.shape[1]
            total = folded_ref.shape[0] // STRIP
            target[...] = jnp.zeros(target.shape, BF)
            for unit in range(n_d * small_rows // STRIP):
                owner, first = (unit * STRIP) // small_rows, (unit * STRIP) % small_rows
                start = pl.multiple_of((owner * experts + dest) * small_rows + first, STRIP)
                target[
                    (unit % total) * STRIP : (unit % total + 1) * STRIP,
                    (unit // total) * wide : (unit // total + 1) * wide,
                ] = small_ref[pl.ds(start, STRIP)]

        last_hop()
        scatter_folded(fold, folded_ref, fold_buffers, fold_semaphores)
        folded_low[...] = folded_ref[...].astype(BF)
        for copy in moves[3 * (n_d - 1) :]:
            copy.start()
        last_sum(sum_ref)
        for copy in moves + outs:
            copy.wait()
        for copy in ride(sources, targets, *ride_sems, start=False):
            copy.wait()


def attention_backward(
    residual_all, output_w, stored, column, row, trig, latent_gain, up_w, first_w, side, gain,
    latent_piece, small_rows, down_now, down_parts, riders, collective_id,
):
    normed, query, key, value, unit, low, scale, attended = stored
    width, rank = residual_all.shape[1], up_w.shape[0]
    rows = row.shape[2]
    n_d = lax.axis_size("dp")
    first_width = 2 * DN + rank
    block = (rows // 2, width)
    folded = (EXTRA_ROWS, width)
    small = (width, rank + 128)
    down_block = (down_now.shape[0] // (2 * LINE), down_now.shape[1])

    def tile(columns):
        return pl.BlockSpec((rows, columns), lambda i: (step_tile(i), 0))

    def fixed(shape):
        return pl.BlockSpec(shape, lambda i: (0, 0), pipeline_mode=pl.Buffered(1))

    anywhere = pl.BlockSpec(memory_space=pl.ANY)
    carried, others = max(1, len(riders)), max(1, n_d - 1)
    query_shape, up_shape, output_shape = (width, 2 * DN), up_w.shape, output_w.shape
    to_others = [
        (n_d - 1, query_shape[0] // n_d, query_shape[1]),
        (n_d - 1, up_shape[0] // n_d, up_shape[1]),
        (n_d - 1, output_shape[0], output_shape[1] // n_d),
        (n_d - 1,) + folded,
    ]
    return pl.pallas_call(
        lambda *refs: attention_backward_kernel(
            latent_piece, small_rows, [rider[1] for rider in riders], *refs
        ),
        grid=(2 * LINE,),
        in_specs=[
            tile(width),
            fixed(output_w.shape),
            tile(DV),
            tile(2 * DN),
            tile(2 * DN),
            tile(DV),
            tile(1),
            pl.BlockSpec((1, 1, rows), lambda i: (step_tile(i), 0, 0)),
            tile(trig.shape[1]),
            tile(rank),
            tile(rank),
            tile(1),
            fixed((1, rank)),
            fixed(up_w.shape),
            tile(width),
            fixed(first_w.shape),
            fixed(side.shape),
            fixed((width, 1)),
            pl.BlockSpec(down_block, lambda i: (i, 0)),
            pl.BlockSpec((n_d - 1,) + down_block, lambda i: (0, i, 0)),
        ]
        + [anywhere] * len(riders),
        out_specs=[
            pl.BlockSpec(block, lambda i: (0, 0)),
            pl.BlockSpec(folded, lambda i: (0, 0)),
            pl.BlockSpec(down_block, lambda i: (i, 0)),
        ]
        + [anywhere] * (7 + len(riders)),
        out_shape=[
            jax.ShapeDtypeStruct(shape, F32)
            for shape in (block, folded, down_now.shape, query_shape, up_shape, output_shape)
        ]
        + [jax.ShapeDtypeStruct(shape, BF) for shape in to_others]
        + [landed(rider) for rider in riders],
        scratch_shapes=[
            pltpu.VMEM((rows, first_width), BF),
            pltpu.VMEM((rows, DN + DV), BF),
            pltpu.VMEM(output_shape, F32),
            pltpu.VMEM(up_shape, F32),
            pltpu.VMEM((width, first_width), F32),
            pltpu.VMEM((1, rank), F32),
            pltpu.VMEM(query_shape, F32),
            pltpu.VMEM(query_shape, BF),
            pltpu.VMEM(up_shape, BF),
            pltpu.VMEM(output_shape, BF),
            pltpu.VMEM(small, BF),
            pltpu.VMEM(folded, BF),
            pltpu.VMEM((2 * LINE,) + folded, BF),
            pltpu.VMEM((2 * LINE,) + folded, BF),
            pltpu.VMEM((LINE + 1,) + folded, BF),
            pltpu.VMEM((LINE + 1,) + folded, BF),
            pltpu.SemaphoreType.DMA((2 * LINE,)),
            pltpu.SemaphoreType.DMA((2 * LINE,)),
            pltpu.SemaphoreType.DMA((LINE,)),
            pltpu.SemaphoreType.DMA((LINE,)),
            pltpu.SemaphoreType.DMA((LINE,)),
            pltpu.SemaphoreType.DMA((LINE + 1,)),
        ]
        + step_buffers(block)
        + [pltpu.SemaphoreType.DMA((carried, others)) for _ in range(2)]
        + [pltpu.SemaphoreType.DMA((3,))]
        + [pltpu.SemaphoreType.DMA((4, others)) for _ in range(2)],
        compiler_params=pltpu.CompilerParams(
            collective_id=collective_id, has_side_effects=True, vmem_limit_bytes=VMEM_LIMIT
        ),
        name="attention_backward",
    )(
        residual_all, output_w, attended, query, key, value, column, row, trig,
        unit, low, scale, latent_gain[None], up_w, normed, first_w, side,
        gain[:, None], down_now, down_parts, *[rider[0] for rider in riders],
    )


HIDDEN = 256
ROUTER_AT = 448


def logistic(values):
    return 0.5 * jnp.tanh(0.5 * values) + 0.5


def expert_layer_kernel(
    splits,
    ffn_ref, y_ref, code_row_ref, code_column_ref, wide_ref, shared_down_ref, *refs,
):
    take = taker(refs)
    own_weights, came = take(3), take(len(splits))
    (
        rows_ref, ups_ref, scaled_ref, gate_ref, up_ref, mixed_ref,
        down_grad_out, wide_grad_out, sum_ref,
    ) = take(9)
    (
        gate_w_ref, up_w_ref, down_w_ref, load_sem, out_sem, down_grad_ref, wide_grad_ref,
        grad_ref, left_ref, inner_ref, returned_ref, slot_gate_ref, slot_dot_ref,
        part, kept, met, paired, passed,
        core_send, core_recv, pair_send, pair_recv, line_send, line_recv,
    ) = take(24)
    step = pl.program_id(0)
    me = lax.axis_index("expert")
    experts = lax.axis_size("expert")
    line, pair, core = place_of(me)
    me_d, n_d = lax.axis_index("dp"), lax.axis_size("dp")
    groups, _, per = code_row_ref.shape
    slots = rows_ref.shape[0] // groups
    width = ffn_ref.shape[1]
    hidden = gate_w_ref.shape[1]

    wholes = (gate_w_ref, up_w_ref, down_w_ref)
    loads = []

    def load(source, number, owner, start, count):
        axis = 1 if number == 2 else 0
        size = own_weights[number].shape[axis]
        at = pl.multiple_of(owner * size, size)
        if axis == 0:
            place = wholes[number].at[pl.ds(at + start, count)]
        else:
            place = wholes[number].at[:, pl.ds(at, size)]
        loads.append(pltpu.make_async_copy(source, place, load_sem.at[len(loads)]))

    for number in range(3):
        load(own_weights[number], number, me_d, 0, own_weights[number].shape[0])
    for source, (number, first, end) in zip(came, splits):
        for ahead in range(1, n_d):
            owner = lax.rem(me_d - ahead + n_d, n_d)
            load(source.at[ahead - 1], number, owner, first, end - first)

    @pl.when(step == 0)
    def _():
        for copy in loads:
            copy.start()
        greet(line, pair, core)
        down_grad_ref[...] = jnp.zeros_like(down_grad_ref)
        wide_grad_ref[...] = jnp.zeros_like(wide_grad_ref)

    out = dot(ffn_ref[...], wide_ref[...])
    gates, ups = out[:, :HIDDEN], out[:, HIDDEN:]
    last = out[:, 2 * HIDDEN - 128 :]
    lane = lax.broadcasted_iota(jnp.int32, last.shape, 1)
    first_lane = ROUTER_AT - (2 * HIDDEN - 128)
    logits = jnp.where((lane >= first_lane) & (lane < first_lane + experts), last, -1e30)
    powers = jnp.exp(logits - jnp.max(logits, axis=1, keepdims=True))
    probs = powers / jnp.sum(powers, axis=1, keepdims=True)
    own_lane = (lane == first_lane + me).astype(F32)
    own_probs = jnp.sum(probs * own_lane, axis=1, keepdims=True)
    sigmoid = logistic(gates)
    silu = gates * sigmoid
    shared_low = (silu * ups).astype(BF)
    back = dot_right(y_ref[...], shared_down_ref[...])
    left_ref[:, :HIDDEN] = (back * ups * sigmoid * (1.0 + gates * (1.0 - sigmoid))).astype(BF)
    shared_up_low = back * silu
    left_ref[:, HIDDEN : 2 * HIDDEN - 128] = shared_up_low[:, : HIDDEN - 128].astype(BF)
    shared_last = shared_up_low[:, HIDDEN - 128 :]
    down_grad_ref[...] += dot_left(shared_low, y_ref[...])

    square = (per, per)
    diagonal = lax.broadcasted_iota(jnp.int32, square, 0) == lax.broadcasted_iota(
        jnp.int32, square, 1
    )
    for group in range(groups):
        tokens_at = pl.ds(group * per, per)
        slots_at = pl.ds(group * slots, slots)
        slot_ids = lax.broadcasted_iota(jnp.int32, (slots, per), 0)
        picks = slot_ids == code_row_ref[group]
        picks_low = picks.astype(F32).astype(BF)
        rows_ref[slots_at] = dot(picks_low, ffn_ref[tokens_at]).astype(BF)
        ups_ref[slots_at] = dot(picks_low, y_ref[tokens_at]).astype(BF)
        own_column = own_probs[group * per : (group + 1) * per]
        own_row = jnp.sum(jnp.where(diagonal, own_column, 0.0), axis=0, keepdims=True)
        slot_gate_ref[slots_at] = jnp.sum(
            jnp.where(picks, own_row, 0.0), axis=1, keepdims=True
        )
    slot_dot_ref[...] = jnp.zeros_like(slot_dot_ref)

    @pl.when(step == 0)
    def _():
        for copy in loads:
            copy.wait()

    def hidden_part(columns):
        gate_part = dot(rows_ref[...], gate_w_ref[:, columns])
        up_part = dot(rows_ref[...], up_w_ref[:, columns])
        raw = dot_right(ups_ref[...], down_w_ref[columns, :])
        slot_gate = slot_gate_ref[...]
        sigmoid = logistic(gate_part)
        silu = gate_part * sigmoid
        inner = silu * up_part
        slot_dot_ref[...] += jnp.sum(inner * raw, axis=1, keepdims=True)
        grad = raw * slot_gate
        inner_ref[:, columns] = inner.astype(BF)
        scaled_ref[:, columns] = (inner * slot_gate).astype(BF)
        gate_ref[:, columns] = (
            grad * up_part * sigmoid * (1.0 + gate_part * (1.0 - sigmoid))
        ).astype(BF)
        up_ref[:, columns] = (grad * silu).astype(BF)

    for first in range(0, hidden, HIDDEN):
        hidden_part(pl.ds(first, min(HIDDEN, hidden - first)))

    @pl.loop(0, width // COLUMNS)
    def _(tile):
        columns = pl.ds(pl.multiple_of(tile * COLUMNS, COLUMNS), COLUMNS)
        returned_ref[:, columns] = dot(inner_ref[...], down_w_ref[:, columns]).astype(BF)
        grad_ref[:, columns] = (
            dot_right(gate_ref[...], gate_w_ref[columns, :])
            + dot_right(up_ref[...], up_w_ref[columns, :])
        ).astype(BF)

    for group in range(groups):
        tokens_at = pl.ds(group * per, per)
        slots_at = pl.ds(group * slots, slots)
        own_column = own_probs[group * per : (group + 1) * per]
        slot_lane = lax.broadcasted_iota(jnp.int32, (per, slots), 1)
        picks = slot_lane == code_column_ref[tokens_at]
        pick_gate = jnp.where(picks, own_column, 0.0).astype(BF)
        mixed_ref[tokens_at] = (
            dot(shared_low[group * per : (group + 1) * per], shared_down_ref[...])
            + dot(pick_gate, returned_ref[slots_at])
        ).astype(BF)
        small = (slots, slots)
        eye = lax.broadcasted_iota(jnp.int32, small, 0) == lax.broadcasted_iota(
            jnp.int32, small, 1
        )
        dot_row = jnp.sum(jnp.where(eye, slot_dot_ref[slots_at], 0.0), axis=0, keepdims=True)
        row_dot = jnp.sum(jnp.where(picks, dot_row, 0.0), axis=1, keepdims=True)
        at = slice(group * per, (group + 1) * per)
        logit_grad = row_dot * own_column * (own_lane[at] - probs[at])
        high = logit_grad.astype(BF)
        rest = logit_grad - high.astype(F32)
        left_ref[tokens_at, 2 * HIDDEN - 128 :] = jnp.where(
            lane[at] < first_lane,
            shared_last[at],
            high.astype(F32) + pltpu.roll(rest, experts, 1),
        ).astype(BF)
    wide_grad_ref[...] += dot_left(ffn_ref[...], left_ref[...])

    advance, finish, _, _ = step_scatter(
        step, (part, kept, met, paired, passed),
        (core_send, core_recv, pair_send, pair_recv, line_send, line_recv),
    )
    rows = kept.shape[0]

    def produce(first, target):
        @pl.loop(0, width // COLUMNS)
        def _(tile):
            columns = pl.ds(pl.multiple_of(tile * COLUMNS, COLUMNS), COLUMNS)
            total = dot_right(left_ref[pl.ds(first, rows)], wide_ref[columns, :])
            for k in range(rows // per):
                group = first // per + k
                slot_lane = lax.broadcasted_iota(jnp.int32, (per, slots), 1)
                picks = slot_lane == code_column_ref[pl.ds(first + k * per, per)]
                scattered = dot(
                    picks.astype(F32).astype(BF),
                    grad_ref[pl.ds(group * slots, slots), columns],
                )
                target[pl.ds(k * per, per), columns] = (
                    total[k * per : (k + 1) * per] + scattered
                ).astype(BF)

    advance(produce)

    @pl.when(step == 2 * LINE - 1)
    def _():
        outs = [
            pltpu.make_async_copy(down_grad_ref, down_grad_out, out_sem.at[0]),
            pltpu.make_async_copy(wide_grad_ref, wide_grad_out, out_sem.at[1]),
        ]
        for copy in outs:
            copy.start()
        finish(sum_ref)
        for copy in outs:
            copy.wait()


def expert_layer(
    ffn_all, upstream_all, code, slots, wide, shared_down, weights, came, splits, collective_id
):
    groups, per = code.shape
    span, width = ffn_all.shape
    gate_w, up_w, down_w = weights
    hidden = gate_w.shape[1]
    n_d = lax.axis_size("dp")
    rows, slot_rows = TILE_GROUPS * per, TILE_GROUPS * slots
    total = groups * slots
    steps = 2 * LINE
    block = (rows // 2, width)

    def tile(count, columns):
        return pl.BlockSpec((count, columns), lambda i: (step_tile(i), 0))

    def fixed(shape):
        return pl.BlockSpec(shape, lambda i: (0, 0), pipeline_mode=pl.Buffered(1))

    anywhere = pl.BlockSpec(memory_space=pl.ANY)
    outs = [(total, width)] * 2 + [(total, hidden)] * 3 + [(span, width)]
    sums = [shared_down.shape, wide.shape]
    copies = 3 + len(came) * (n_d - 1)
    return pl.pallas_call(
        lambda *refs: expert_layer_kernel(splits, *refs),
        grid=(steps,),
        in_specs=[
            tile(rows, width),
            tile(rows, width),
            pl.BlockSpec((TILE_GROUPS, 1, per), lambda i: (step_tile(i), 0, 0)),
            tile(rows, 1),
            fixed(wide.shape),
            fixed(shared_down.shape),
        ]
        + [anywhere] * (3 + len(came)),
        out_specs=[
            tile(slot_rows if shape[0] == total else rows, shape[1]) for shape in outs
        ]
        + [anywhere] * 2
        + [pl.BlockSpec(block, lambda i: (0, 0))],
        out_shape=[jax.ShapeDtypeStruct(shape, BF) for shape in outs]
        + [jax.ShapeDtypeStruct(shape, F32) for shape in sums]
        + [jax.ShapeDtypeStruct(block, BF)],
        scratch_shapes=[
            pltpu.VMEM((gate_w.shape[0] * n_d, hidden), BF),
            pltpu.VMEM((up_w.shape[0] * n_d, hidden), BF),
            pltpu.VMEM((hidden, down_w.shape[1] * n_d), BF),
            pltpu.SemaphoreType.DMA((copies,)),
            pltpu.SemaphoreType.DMA((2,)),
            pltpu.VMEM(shared_down.shape, F32),
            pltpu.VMEM(wide.shape, F32),
            pltpu.VMEM((slot_rows, width), BF),
            pltpu.VMEM((rows, 2 * HIDDEN), BF),
            pltpu.VMEM((slot_rows, hidden), BF),
            pltpu.VMEM((slot_rows, width), BF),
            pltpu.VMEM((slot_rows, 1), F32),
            pltpu.VMEM((slot_rows, 1), F32),
        ]
        + step_buffers(block),
        compiler_params=pltpu.CompilerParams(
            collective_id=collective_id,
            has_side_effects=True,
            vmem_limit_bytes=63 * 1024 * 1024,
        ),
        name="expert_layer",
    )(
        ffn_all, upstream_all, code[:, None, :], code.reshape(span, 1), wide, shared_down,
        gate_w, up_w, down_w, *came,
    )


def on_device(
    tokens,
    segment,
    routes,
    drop_order,
    cotangent,
    attn_gain,
    query_weight,
    down_latent,
    latent_gain,
    up_latent,
    output_weight,
    ffn_gain,
    router_weight,
    shared_gate,
    shared_up,
    shared_down,
    expert_gate,
    expert_up,
    expert_down,
):
    n_e = lax.axis_size("expert")
    n_d = lax.axis_size("dp")
    me_e = lax.axis_index("expert")
    me_d = lax.axis_index("dp")
    micro, group_rows, width = tokens.shape
    own_rows = micro * group_rows
    span = n_e * own_rows
    groups = n_e * micro
    top = routes.shape[2]
    experts = n_e * expert_gate.shape[0]
    capacity = (5 * group_rows * top + 4 * experts - 1) // (4 * experts)
    slots = -(-capacity // 16) * 16
    rank_latent = latent_gain.shape[0] * n_e * n_d

    def gather(values):
        return lax.all_gather(values, "expert", axis=0, tiled=True)

    def scatter(values):
        return lax.psum_scatter(values, "expert", scatter_dimension=0, tiled=True)

    def whole(own, parts, axis):
        blocks = [own] + [parts[step - 1] for step in range(1, n_d)]
        ordered = [
            lax.select_n(lax.rem(me_d - owner + n_d, n_d), *blocks) for owner in range(n_d)
        ]
        return jnp.concatenate(ordered, axis=axis)

    def split_dp(values, axis):
        size = values.shape[axis] // n_d
        parts = []
        for step in range(n_d):
            at = lax.rem(me_d + step, n_d) * size
            parts.append(lax.dynamic_slice_in_dim(values, at, size, axis))
        return (stack([part.astype(BF) for part in parts[1:]]), parts[0])

    def stack(parts):
        return parts[0][None] if len(parts) == 1 else jnp.stack(parts)

    def add_all(total, parts):
        for step in range(n_d - 1):
            total = total + parts[step].astype(F32)
        return total

    small_rows = attn_gain.shape[0]
    latent_all_width = down_latent.shape[1]
    latent_piece = latent_gain.shape[0]
    packed = jnp.concatenate(
        [
            down_latent,
            router_weight,
            attn_gain[:, None],
            ffn_gain[:, None],
            jnp.pad(latent_gain, (0, small_rows - latent_piece))[:, None],
        ],
        axis=1,
    )
    packed = lax.all_gather(packed, ("dp", "expert"), axis=0, tiled=True)
    down_all = packed[:, :latent_all_width]
    router_all = packed[:, latent_all_width : latent_all_width + experts]
    rest = packed[:, latent_all_width + experts :].astype(F32)
    attn_gain_all = rest[:, 0]
    ffn_gain_all = rest[:, 1]
    latent_gain_all = rest[:, 2].reshape(n_e * n_d, small_rows)[:, :latent_piece].reshape(-1)

    chosen = jnp.sum(
        (routes[..., None] == jnp.arange(experts, dtype=jnp.int32)).astype(jnp.int32), axis=2
    )
    order = drop_order[:, 0]
    earlier = (order[:, None, :] < order[:, :, None]).astype(F32)
    rank = jnp.einsum("mtu,mue->mte", earlier, chosen.astype(F32)).astype(jnp.int32)
    code = jnp.where((chosen == 1) & (rank < capacity), rank, -1).reshape(own_rows, experts)

    tokens_own = tokens.reshape(own_rows, width)
    code_lanes = -(-experts // 128) * 128
    code_low = jnp.pad(code.astype(BF), ((0, 0), (0, code_lanes - experts)))
    own_gate, own_up, own_down = expert_gate[0], expert_up[0], expert_down[0]
    gate_first = own_gate.shape[0] // 4
    dense = (query_weight, up_latent, output_weight, shared_gate, shared_up, shared_down)
    came = gather_rows(
        jnp.concatenate([tokens_own, code_low], axis=1),
        5,
        riders=[(array, (0, array.shape[0])) for array in dense] + [(own_gate, (0, gate_first))],
    )
    tokens_all, gate_came = came[0], came[7]
    query_w, up_w, output_w, shared_gate_w, shared_up_w, shared_down_w = [
        whole(own, parts, axis)
        for own, parts, axis in zip(dense, came[1:7], (0, 0, 1, 0, 0, 1))
    ]
    upstream_own = cotangent.reshape(own_rows, width)
    upstream_later, tokens_all = lax.optimization_barrier((upstream_own, tokens_all))
    upstream_all = gather(upstream_later)
    code_all = tokens_all[:, width : width + experts].astype(jnp.int32)
    my_code = lax.dynamic_slice_in_dim(code_all, me_e, 1, 1).reshape(groups, group_rows)

    span_segment = (
        segment.reshape(micro, n_e, group_rows).transpose(1, 0, 2).reshape(groups, group_rows)
    )
    trig = angles(positions(span_segment), group_rows)
    marks = span_segment + 4 * jnp.arange(groups, dtype=jnp.int32)[:, None]
    column = marks.reshape(span, 1)
    row = marks.reshape(groups // TILE_GROUPS, 1, TILE_GROUPS * group_rows)
    first_w = jnp.concatenate(
        [
            query_w[:, :DN],
            down_all[:, :rank_latent],
            down_all[:, rank_latent:],
            query_w[:, DN:],
        ],
        axis=1,
    )
    came = attention_forward(
        tokens_all,
        attn_gain_all,
        first_w,
        latent_gain_all,
        up_w,
        trig,
        column,
        row,
        output_w,
        [(own_gate, (gate_first, own_gate.shape[0])), (own_up, (0, own_up.shape[0]))],
        2,
    )
    stored, attention_out, gate_came_last, up_came = came[:8], came[8], came[9], came[10]
    residual = tokens_own.astype(F32) + attention_out

    second_scale = rms_scale(residual)
    ffn_in = (residual * second_scale * ffn_gain_all).astype(BF)
    ffn_all, down_came = gather_rows(ffn_in, 1, riders=[(own_down, (0, own_down.shape[0]))])

    shared_hidden = shared_gate_w.shape[1]
    wide = jnp.concatenate(
        [
            jnp.pad(shared_gate_w, ((0, 0), (0, HIDDEN - shared_hidden))),
            jnp.pad(shared_up_w, ((0, 0), (0, ROUTER_AT - HIDDEN - shared_hidden))),
            router_all,
            jnp.pad(router_all, ((0, 0), (0, 2 * HIDDEN - ROUTER_AT - 2 * experts))),
        ],
        axis=1,
    )
    (
        expert_rows,
        slot_up,
        inner_scaled,
        gate_low,
        up_low,
        mixed_part,
        shared_down_grad,
        wide_grad,
        ffn_grad,
    ) = expert_layer(
        ffn_all,
        upstream_all,
        my_code,
        slots,
        wide,
        jnp.pad(shared_down_w, ((0, HIDDEN - shared_hidden), (0, 0))),
        (own_gate, own_up, own_down),
        (gate_came, gate_came_last, up_came, down_came),
        (
            (0, 0, gate_first),
            (0, gate_first, own_gate.shape[0]),
            (1, 0, own_up.shape[0]),
            (2, 0, own_down.shape[0]),
        ),
        3,
    )
    ffn_grad = ffn_grad.astype(F32)
    mixed = residual + scatter(mixed_part).astype(F32)
    router_grad = (
        wide_grad[:, ROUTER_AT : ROUTER_AT + experts]
        + wide_grad[:, ROUTER_AT + experts : ROUTER_AT + 2 * experts]
    )
    shared_down_later, shared_down_now = split_dp(shared_down_grad[:shared_hidden], 1)
    shared_gate_later, shared_gate_now = split_dp(wide_grad[:, :shared_hidden], 0)
    shared_up_later, shared_up_now = split_dp(wide_grad[:, HIDDEN : HIDDEN + shared_hidden], 0)
    residual_part, ffn_gain_grad = norm_back(residual, second_scale, ffn_gain_all, ffn_grad)
    residual_grad = upstream_own.astype(F32) + residual_part
    (
        residual_all,
        shared_down_parts,
        shared_gate_parts,
        shared_up_parts,
        down_now,
        gate_now,
        up_now,
        down_parts,
        gate_parts_first,
        gate_later,
        up_later,
    ) = gather_rows(
        residual_grad.astype(BF),
        6,
        riders=[
            (later, None) for later in (shared_down_later, shared_gate_later, shared_up_later)
        ],
        products=(expert_rows, slot_up, inner_scaled, gate_low, up_low),
    )

    side = jnp.concatenate(
        [
            jnp.zeros((width, DR), F32),
            router_grad,
            ffn_gain_grad[:, None],
            jnp.zeros((width, 128 - DR - experts - 1), F32),
        ],
        axis=1,
    ).astype(BF)
    (
        normed_grad,
        folded,
        down_grad,
        query_full,
        up_latent_full,
        output_full,
        query_parts,
        latent_parts,
        output_parts,
        folded_parts,
        gate_parts_last,
        up_parts,
    ) = attention_backward(
        residual_all,
        output_w,
        stored,
        column,
        row,
        trig,
        latent_gain_all,
        up_w,
        first_w,
        side,
        attn_gain_all,
        latent_piece,
        small_rows,
        down_now,
        down_parts,
        [(gate_later, None), (up_later, None)],
        4,
    )

    def own_part(values, axis):
        size = values.shape[axis] // n_d
        return lax.dynamic_slice_in_dim(values, me_d * size, size, axis)

    query_grad = add_all(own_part(query_full, 0), query_parts)[:, : DN + DR]
    up_latent_grad = add_all(own_part(up_latent_full, 0), latent_parts)
    output_grad = add_all(own_part(output_full, 1), output_parts)
    small_width = rank_latent + 128
    folded = add_all(folded, folded_parts)
    small = jnp.concatenate(
        [folded[:, k * small_width : (k + 1) * small_width] for k in range(width // small_width)],
        axis=0,
    )
    small = lax.dynamic_slice_in_dim(small, me_d * small_rows, small_rows, 0)
    own_inputs = tokens_own.astype(F32)
    input_part, _ = norm_back(own_inputs, rms_scale(own_inputs), attn_gain_all, normed_grad)
    tokens_grad = residual_grad + input_part
    last = latent_all_width + experts
    shape = (micro, group_rows, width)
    return (
        mixed.reshape(shape),
        tokens_grad.reshape(shape),
        small[:, last + 1],
        query_grad,
        small[:, :latent_all_width],
        small[:latent_piece, last + 2],
        up_latent_grad,
        output_grad,
        small[:, last],
        small[:, latent_all_width:last],
        add_all(shared_gate_now, shared_gate_parts),
        add_all(shared_up_now, shared_up_parts),
        add_all(shared_down_now, shared_down_parts),
        jnp.concatenate(
            [
                add_all(gate_now[: gate_now.shape[0] // 2], gate_parts_first),
                add_all(gate_now[gate_now.shape[0] // 2 :], gate_parts_last),
            ],
            axis=0,
        )[None],
        add_all(up_now, up_parts)[None],
        down_grad[None],
    )


def solution(mesh):
    rows = P(None, ("dp", "expert"), None)
    split = P(("dp", "expert"))
    split_rows = P(("dp", "expert"), None)
    columns = P("dp", "expert")
    turned = P("expert", "dp")
    expert_in = P("expert", "dp", None)
    expert_out = P("expert", None, "dp")
    return jax.shard_map(
        on_device,
        mesh=mesh,
        in_specs=(
            rows,
            P(None, "dp"),
            rows,
            rows,
            rows,
            split,
            columns,
            split_rows,
            split,
            columns,
            turned,
            split,
            split_rows,
            columns,
            columns,
            turned,
            expert_in,
            expert_in,
            expert_out,
        ),
        out_specs=(
            rows,
            rows,
            split,
            columns,
            split_rows,
            split,
            columns,
            turned,
            split,
            split_rows,
            columns,
            columns,
            turned,
            expert_in,
            expert_in,
            expert_out,
        ),
        check_vma=False,
    )
```

profile of v0, /device:TPU:0, one launch (start us, length us, event | category | flops | bytes accessed | tf_op | source)
XLA Modules:
  0.0 859.7 jit_solution(12480292470606962275)
XLA Ops:
  13.9 2.0 copy.105.refs_1_
  15.9 2.0 copy.106.refs_4_
  19.9 90.5 %gather_rows.3 = (bf16[16,192,2176]{2,1,0:T(8,128)(2,1)}, bf16[1,1024,192]{2,1,0:T(8,128)(2,1)}, bf16[1,256,256]{2,1,0:T(8,128)(2,1)}, bf16[1,128,1024]{2,1,0:T(...) custom-call(bf16[192,2176]{1,0:T(8,128)(2,1)} %fusion.31.refs_0_, ...), custom_call_target="tpu_custom_call" | custom-call | tf_op jit(solution)/shard_map/gather_rows/pallas_call | solution.py:404
  125.8 3.6 fusion.27.refs_5_.refs_8_
  132.1 2.6 slice_reduce_fusion
  135.4 6.4 fusion.5.refs_2_.refs_15_
  141.8 120.0 %attention_forward.1 = (bf16[3072,2048]{1,0:T(8,128)(2,1)}, bf16[3072,256]{1,0:T(8,128)(2,1)}, bf16[3072,256]{1,0:T(8,128)(2,1)}, bf16[3072,128]{1,0:T(8,128)(2,...) custom-call(bf16[3072,2176]{1,0:T(8,128)(2,1)} %bitcast.100, ...), custom_call_target="tpu_custom_call" | custom-call | tf_op jit(solution)/shard_map/attention_forward/pallas_call | solution.py:827
  265.7 73.4 %gather_rows.4 = (bf16[16,192,2048]{2,1,0:T(8,128)(2,1)}, bf16[1,1408,1024]{2,1,0:T(8,128)(2,1)}) custom-call(bf16[192,2048]{1,0:T(8,128)(2,1)} %multiply_convert_fusion.refs_0_, bf16[1408,1024]{1,0:T(8,128)(2,1)} %bitcast.103), custom_call_target="tpu_custom_call" | custom-call | tf_op jit(solution)/shard_map/gather_rows/pallas_call | solution.py:404
  339.4 3.4 fusion.6.refs_4_
  342.8 183.9 %expert_layer.1 = (bf16[1536,2048]{1,0:T(8,128)(2,1)}, bf16[1536,2048]{1,0:T(8,128)(2,1)}, bf16[1536,1408]{1,0:T(8,128)(2,1)}, bf16[1536,1408]{1,0:T(8,128)(2,1)...) custom-call(bf16[3072,2048]{1,0:T(8,128)(2,1)} %bitcast.102, ...), custom_call_target="tpu_custom_call" | custom-call | tf_op jit(solution)/shard_map/expert_layer/pallas_call | solution.py:1354
  535.6 139.9 %gather_rows.5 = (bf16[16,192,2048]{2,1,0:T(8,128)(2,1)}, bf16[1,176,1024]{2,1,0:T(8,128)(2,1)}, bf16[1,1024,176]{2,1,0:T(8,128)(2,1)}, bf16[1,1024,176]{2,1,0:T...) custom-call(bf16[192,2048]{1,0:T(8,128)(2,1)} %fusion.51.refs_0_, ...), custom_call_target="tpu_custom_call" | custom-call | tf_op jit(solution)/shard_map/gather_rows/pallas_call | solution.py:404
  675.6 2.4 convert_add_fusion.5
  678.0 2.4 copy.126
  680.4 2.5 convert_add_fusion.6
  682.9 2.4 copy.125
  685.3 2.3 add_convert_fusion
  689.0 127.6 %attention_backward.1 = (f32[192,2048]{1,0:T(8,128)}, f32[48,2048]{1,0:T(8,128)}, f32[1408,1024]{1,0:T(8,128)}, f32[2048,256]{1,0:T(8,128)}, f32[512,256]{1,0:T(...) custom-call(bf16[3072,2048]{1,0:T(8,128)(2,1)} %bitcast.101, ...), custom_call_target="tpu_custom_call" | custom-call | tf_op jit(solution)/shard_map/attention_backward/pallas_call | solution.py:1051
  818.5 2.4 dynamic-slice_add_fusion
  820.9 2.5 copy.123
  830.3 3.2 convert_add_fusion.2
  833.6 3.3 maximum_bitcast_fusion
  839.2 3.0 fusion.2
  842.2 4.6 fusion.25
  846.8 6.2 copy.133
  (181 shorter events, 52.6 us)
Async XLA Ops:
  7.2 10.7 %copy-start.29 = (bf16[1024,176]{0,1:T(8,128)(2,1)S(1)}, bf16[1024,176]{0,1:T(8,128)(2,1)}, u32[]{:S(2)}) copy-start(bf16[1024,176]{0,1:T(8,128)(2,1)} %param.33) | copy-start | bytes 1081348
  7.2 11.7 %copy-start.2 = (bf16[2,96,2048]{2,1,0:T(8,128)(2,1)S(1)}, bf16[2,96,2048]{2,1,0:T(8,128)(2,1)}, u32[]{:S(2)}) copy-start(bf16[2,96,2048]{2,1,0:T(8,128)(2,1)} %param.19) | copy-start | bytes 2359300
  7.2 123.6 %all-gather.3.cloned.1.call-start = ((), (), s32[]{:S(2)}) async-start(), calls=%async_computation.1 | async-start | bytes 2703360 | tf_op jit(solution)/shard_map/all_gather | solution.py:1479
  12.1 330.7 %all-gather.5.cloned.1.call-start = ((), (), s32[]{:S(2)}) async-start(), calls=%async_computation.2 | async-start | bytes 13369344 | tf_op jit(solution)/shard_map/all_gather | solution.py:1438
  19.9 90.6 %copy-start.38 = (s32[2,1536]{1,0:T(2,128)S(1)}, s32[2,1536]{1,0:T(2,128)}, u32[]{:S(2)}) copy-start(s32[2,1536]{1,0:T(2,128)} %param.20) | copy-start | bytes 36868
  110.4 731.8 %reduce-scatter.2.cloned.1.call-start = ((), (), s32[]{:S(2)}) async-start(), calls=%async_computation.3 | async-start | bytes 13369344 | tf_op jit(solution)/shard_map/reduce_scatter | solution.py:1441
  113.2 5.3 copy-start.26
  113.2 5.3 copy-start.35
  114.8 4.5 copy-start.14
  114.8 4.5 copy-start.27
  531.6 4.0 copy-start.7
  531.6 4.0 copy-start.8
  817.7 6.4 copy-start.28
  818.5 6.3 copy-start.37
  820.9 5.7 copy-start.36
  823.4 5.1 copy-start.32
  823.4 5.1 copy-start.34
  824.8 4.6 copy-start.16
  824.8 4.6 copy-start.31
  826.6 3.7 copy-start.19
  826.6 3.7 copy-start.20
  833.5 4.3 slice-start
  833.5 4.8 slice-start.1
  833.5 5.6 copy-start.17
  (20 other events, 40.8 us)
Sparse Core Ops, SparseCore 0:
  12.2 67.7 all-gather.2
  110.5 141.3 all-gather.4
  526.9 166.3 reduce-scatter.1
where the time goes:
time: 872 us; the launch traced here: 860 us
  Pallas kernels  735 us (84%)
  other arithmetic  59.6 us (7%)
  local copies, waits for them, and re-layouts  45.5 us (5%)
  between operations  14.6 us (2%)
    pallas_call x3, Pallas kernels, gather_rows(): pl.pallas_call(lambda *refs: gather_kernel([rider[1] for rider in riders]...  304 us
    pallas_call x1, Pallas kernels, expert_layer(): pl.pallas_call(lambda *refs: expert_layer_kernel(splits, *refs), grid=(st...  184 us
    pallas_call x1, Pallas kernels, attention_backward(): pl.pallas_call(lambda *refs: attention_backward_kernel(latent_piece, smal...  128 us
    pallas_call x1, Pallas kernels, attention_forward(): pl.pallas_call(lambda *refs: attention_forward_kernel([rider[1] for rider...  120 us
    unnamed x92, local copies, waits for them, and re-layouts  27.1 us
  transfers between devices with their start and end apart: 3, of which 0 were waited for; matrix products, arithmetic and copies ran while one was open for 10% of the time, Pallas kernels for 64%

commit v1 on v0

--- a/solution.py
+++ b/solution.py
@@ -1496,7 +1496,8 @@
     code_lanes = -(-experts // 128) * 128
     code_low = jnp.pad(code.astype(BF), ((0, 0), (0, code_lanes - experts)))
     own_gate, own_up, own_down = expert_gate[0], expert_up[0], expert_down[0]
-    gate_first = own_gate.shape[0] // 4
+    gate_first = own_gate.shape[0] * 3 // 8
+    up_most = own_up.shape[0] * 7 // 8
     dense = (query_weight, up_latent, output_weight, shared_gate, shared_up, shared_down)
     came = gather_rows(
         jnp.concatenate([tokens_own, code_low], axis=1),
@@ -1540,7 +1541,7 @@
         column,
         row,
         output_w,
-        [(own_gate, (gate_first, own_gate.shape[0])), (own_up, (0, own_up.shape[0]))],
+        [(own_gate, (gate_first, own_gate.shape[0])), (own_up, (0, up_most))],
         2,
     )
     stored, attention_out, gate_came_last, up_came = came[:8], came[8], came[9], came[10]
@@ -1548,7 +1549,11 @@
 
     second_scale = rms_scale(residual)
     ffn_in = (residual * second_scale * ffn_gain_all).astype(BF)
-    ffn_all, down_came = gather_rows(ffn_in, 1, riders=[(own_down, (0, own_down.shape[0]))])
+    ffn_all, up_came_last, down_came = gather_rows(
+        ffn_in,
+        1,
+        riders=[(own_up, (up_most, own_up.shape[0])), (own_down, (0, own_down.shape[0]))],
+    )
 
     shared_hidden = shared_gate_w.shape[1]
     wide = jnp.concatenate(
@@ -1578,11 +1583,12 @@
         wide,
         jnp.pad(shared_down_w, ((0, HIDDEN - shared_hidden), (0, 0))),
         (own_gate, own_up, own_down),
-        (gate_came, gate_came_last, up_came, down_came),
+        (gate_came, gate_came_last, up_came, up_came_last, down_came),
         (
             (0, 0, gate_first),
             (0, gate_first, own_gate.shape[0]),
-            (1, 0, own_up.shape[0]),
+            (1, 0, up_most),
+            (1, up_most, own_up.shape[0]),
             (2, 0, own_down.shape[0]),
         ),
         3,
@@ -1694,13 +1700,7 @@
         add_all(shared_gate_now, shared_gate_parts),
         add_all(shared_up_now, shared_up_parts),
         add_all(shared_down_now, shared_down_parts),
-        jnp.concatenate(
-            [
-                add_all(gate_now[: gate_now.shape[0] // 2], gate_parts_first),
-                add_all(gate_now[gate_now.shape[0] // 2 :], gate_parts_last),
-            ],
-            axis=0,
-        )[None],
+        add_all(gate_now, jnp.concatenate([gate_parts_first, gate_parts_last], axis=1))[None],
         add_all(up_now, up_parts)[None],
         down_grad[None],
     )

time: 872 us -> 870 us (level)
  transfers between devices with their start and end apart: 3 -> 3, of which waited for: 0 -> 0; matrix products, arithmetic and copies ran while one was open for 10% -> 10% of each run, Pallas kernels for 64% -> 65%
where the time goes in v1:
time: 870 us; the launch traced here: 861 us
  Pallas kernels  738 us (85%)
  other arithmetic  59.3 us (7%)
  local copies, waits for them, and re-layouts  44.3 us (5%)
  between operations  14.6 us (2%)
    pallas_call x3, Pallas kernels, gather_rows(): pl.pallas_call(lambda *refs: gather_kernel([rider[1] for rider in riders]...  308 us
    pallas_call x1, Pallas kernels, expert_layer(): pl.pallas_call(lambda *refs: expert_layer_kernel(splits, *refs), grid=(st...  182 us
    pallas_call x1, Pallas kernels, attention_backward(): pl.pallas_call(lambda *refs: attention_backward_kernel(latent_piece, smal...  128 us
    pallas_call x1, Pallas kernels, attention_forward(): pl.pallas_call(lambda *refs: attention_forward_kernel([rider[1] for rider...  120 us
    unnamed x92, local copies, waits for them, and re-layouts  25.9 us
  transfers between devices with their start and end apart: 3, of which 0 were waited for; matrix products, arithmetic and copies ran while one was open for 10% of the time, Pallas kernels for 65%

profile of v1, /device:TPU:0, one launch (start us, length us, event | category | flops | bytes accessed | tf_op | source)
XLA Modules:
  0.0 860.7 jit_solution(14727508675584984447)
XLA Ops:
  13.9 2.0 copy.105.refs_1_
  15.9 2.0 copy.106.refs_4_
  19.9 90.5 %gather_rows.3 = (bf16[16,192,2176]{2,1,0:T(8,128)(2,1)}, bf16[1,1024,192]{2,1,0:T(8,128)(2,1)}, bf16[1,256,256]{2,1,0:T(8,128)(2,1)}, bf16[1,128,1024]{2,1,0:T(...) custom-call(bf16[192,2176]{1,0:T(8,128)(2,1)} %fusion.32.refs_0_, ...), custom_call_target="tpu_custom_call" | custom-call | tf_op jit(solution)/shard_map/gather_rows/pallas_call | solution.py:404
  125.8 3.6 fusion.28.refs_5_.refs_8_
  132.1 2.6 slice_reduce_fusion
  135.4 6.4 fusion.6.refs_2_.refs_15_
  141.8 120.1 %attention_forward.1 = (bf16[3072,2048]{1,0:T(8,128)(2,1)}, bf16[3072,256]{1,0:T(8,128)(2,1)}, bf16[3072,256]{1,0:T(8,128)(2,1)}, bf16[3072,128]{1,0:T(8,128)(2,...) custom-call(bf16[3072,2176]{1,0:T(8,128)(2,1)} %bitcast.102, ...), custom_call_target="tpu_custom_call" | custom-call | tf_op jit(solution)/shard_map/attention_forward/pallas_call | solution.py:827
  265.8 76.6 %gather_rows.4 = (bf16[16,192,2048]{2,1,0:T(8,128)(2,1)}, bf16[1,128,1408]{2,1,0:T(8,128)(2,1)}, bf16[1,1408,1024]{2,1,0:T(8,128)(2,1)}) custom-call(bf16[192,2048]{1,0:T(8,128)(2,1)} %multiply_convert_fusion.refs_0_, bf16[1024,1408]{1,0:T(8,128)(2,1)} %bitcast.96, bf16[1408,1024]{1,0:T(8,128)(2,1)} %bitcast.105), custom_call_target="tpu_custom_call" | custom-call | tf_op jit(solution)/shard_map/gather_rows/pallas_call | solution.py:404
  342.6 3.4 fusion.7.refs_4_
  346.1 182.0 %expert_layer.1 = (bf16[1536,2048]{1,0:T(8,128)(2,1)}, bf16[1536,2048]{1,0:T(8,128)(2,1)}, bf16[1536,1408]{1,0:T(8,128)(2,1)}, bf16[1536,1408]{1,0:T(8,128)(2,1)...) custom-call(bf16[3072,2048]{1,0:T(8,128)(2,1)} %bitcast.104, ...), custom_call_target="tpu_custom_call" | custom-call | tf_op jit(solution)/shard_map/expert_layer/pallas_call | solution.py:1354
  537.0 141.0 %gather_rows.5 = (bf16[16,192,2048]{2,1,0:T(8,128)(2,1)}, bf16[1,176,1024]{2,1,0:T(8,128)(2,1)}, bf16[1,1024,176]{2,1,0:T(8,128)(2,1)}, bf16[1,1024,176]{2,1,0:T...) custom-call(bf16[192,2048]{1,0:T(8,128)(2,1)} %fusion.52.refs_0_, ...), custom_call_target="tpu_custom_call" | custom-call | tf_op jit(solution)/shard_map/gather_rows/pallas_call | solution.py:404
  678.0 2.4 convert_add_fusion.4
  680.5 2.4 copy.126
  682.9 2.5 convert_add_fusion.5
  685.3 2.4 copy.125
  687.8 2.3 add_convert_fusion
  691.4 127.6 %attention_backward.1 = (f32[192,2048]{1,0:T(8,128)}, f32[48,2048]{1,0:T(8,128)}, f32[1408,1024]{1,0:T(8,128)}, f32[2048,256]{1,0:T(8,128)}, f32[512,256]{1,0:T(...) custom-call(bf16[3072,2048]{1,0:T(8,128)(2,1)} %bitcast.103, ...), custom_call_target="tpu_custom_call" | custom-call | tf_op jit(solution)/shard_map/attention_backward/pallas_call | solution.py:1051
  821.0 2.4 dynamic-slice_add_fusion
  823.4 2.5 copy.123
  829.1 1.8 convert_add_fusion.9
  832.9 6.2 fusion.3
  840.2 3.0 fusion.2
  843.2 4.6 fusion.26
  847.8 6.2 copy.133
  (180 shorter events, 49.6 us)
Async XLA Ops:
  7.2 10.7 %copy-start.29 = (bf16[1024,176]{0,1:T(8,128)(2,1)S(1)}, bf16[1024,176]{0,1:T(8,128)(2,1)}, u32[]{:S(2)}) copy-start(bf16[1024,176]{0,1:T(8,128)(2,1)} %param.33) | copy-start | bytes 1081348
  7.2 11.7 %copy-start.2 = (bf16[2,96,2048]{2,1,0:T(8,128)(2,1)S(1)}, bf16[2,96,2048]{2,1,0:T(8,128)(2,1)}, u32[]{:S(2)}) copy-start(bf16[2,96,2048]{2,1,0:T(8,128)(2,1)} %param.19) | copy-start | bytes 2359300
  7.2 123.6 %all-gather.3.cloned.1.call-start = ((), (), s32[]{:S(2)}) async-start(), calls=%async_computation.1 | async-start | bytes 2703360 | tf_op jit(solution)/shard_map/all_gather | solution.py:1479
  12.1 334.0 %all-gather.5.cloned.1.call-start = ((), (), s32[]{:S(2)}) async-start(), calls=%async_computation.2 | async-start | bytes 13369344 | tf_op jit(solution)/shard_map/all_gather | solution.py:1438
  19.9 90.6 %copy-start.38 = (s32[2,1536]{1,0:T(2,128)S(1)}, s32[2,1536]{1,0:T(2,128)}, u32[]{:S(2)}) copy-start(s32[2,1536]{1,0:T(2,128)} %param.20) | copy-start | bytes 36868
  110.4 732.8 %reduce-scatter.2.cloned.1.call-start = ((), (), s32[]{:S(2)}) async-start(), calls=%async_computation.3 | async-start | bytes 13369344 | tf_op jit(solution)/shard_map/reduce_scatter | solution.py:1441
  113.2 5.3 copy-start.26
  113.2 5.3 copy-start.35
  114.8 4.5 copy-start.14
  114.8 4.5 copy-start.27
  533.0 4.0 copy-start.7
  533.0 4.0 copy-start.8
  820.2 6.4 copy-start.28
  821.0 6.3 copy-start.37
  823.4 5.7 copy-start.36
  825.9 5.1 copy-start.32
  825.9 5.1 copy-start.34
  827.3 4.6 copy-start.16
  827.3 4.6 copy-start.31
  829.1 3.7 copy-start.19
  829.1 3.7 copy-start.20
  832.8 6.2 slice-start
  832.8 6.2 slice-start.1
  832.8 7.3 copy-start.17
  (20 other events, 40.9 us)
Sparse Core Ops, SparseCore 0:
  12.2 67.7 all-gather.2
  110.5 141.3 all-gather.4
  528.3 171.9 reduce-scatter.1
